TPU v7x, 128 devices: a whole 4x4x4 slice. The times are simulated.
128 devices in a mesh: dp: 32 (over z, y, core), group: 4 (over x).
Axes of the slice: x: 4, y: 4, z: 4, core: 2. Of those that a mesh axis runs over, the one named last changes fastest.
Arguments:
- hidden_in: bfloat16 [256, 128, 1024], P(('dp', 'group')), may hold values from -6 to 6
- out_grad: bfloat16 [256, 128, 1024], P(('dp', 'group')), may hold values from -6 to 6
- seq_owner: int32 [160], replicated, may hold values from 0 to 127, as said below
- token_place: int32 [256, 128], P(('dp', 'group')), may hold values from 0 to 4603, as said below
- matrix_slot: int32 [7], replicated, may hold values from 0 to 7, as said below
- weight_slots: float32 [8, 1024, 3072], P('group', 'dp'), may hold values from -1 to 1
- momentum_slots: float32 [8, 1024, 3072], P('group', 'dp'), may hold values from -448 to 448
- gains: float32 [2304], replicated, may hold values from 0.8 to 6
- gain_momentum: float32 [2304], replicated, may hold values from -448 to 448
Outputs:
- hidden_out: bfloat16 [256, 128, 1024], P(('dp', 'group'))
- in_grad: float32 [256, 128, 1024], P(('dp', 'group'))
- weight_grad: float32 [8, 1024, 3072], P('group', 'dp')
- momentum_new: float32 [8, 1024, 3072], P('group', 'dp')
- weight_new: float32 [8, 1024, 3072], P('group', 'dp')
- gain_grad: float32 [2304], replicated
- gain_momentum_new: float32 [2304], replicated
- gain_new: float32 [2304], replicated
Inputs may be any that keep to these rules, and one draw needn't show every extreme that they name: `seq_owner`: not falling; each replica is named 1 or 2 times, exactly 32 of them 2 times; a replica's sequences fill its first slots. `token_place`: strictly rising along each slot's tokens, by 1 to 4 from one token to the next. `matrix_slot`: seven distinct slots, for the query, key, value, output, gate, up and down projections in this order; slot s belongs to group index s // 2.
All inputs are finite; a program needn't handle non-finite values.
Results may differ from a plain program's by a relative error of at most 0.029.
Values may be sent and summed in bfloat16 or wider, within the bound.
No kernel may reach another device: no remote copies, remote signals or barrier semaphores. Data moves between devices by JAX's collectives and lax.ppermute only.
A program may use at most 320 MiB of HBM per device.

v0:
```python
import jax
import jax.numpy as jnp
from jax import lax
from jax.sharding import Mesh
from jax.sharding import PartitionSpec as P

D = 1024
HEADS = 16
KV = 8
HD = 128
FF = 3072
NS_ITERS = 5
DP = ("dp_0", "dp_1", "dp_2")
DP_GROUP = ("dp_0", "dp_1", "dp_2", "group")


norm_eps = 1e-06
frob_eps = 1e-07
rope_base = 1000000.0
coef_linear = 3.4445
coef_square = -4.775
coef_quartic = 2.0315
momentum_keep = 0.95
learn_rate = 0.15
weight_decay = 0.1
gain_rate = 0.5
masked_score = -1e30


def joined_along(pieces, dim):
    lengths = list(pieces.shape[1:])
    lengths[dim] *= pieces.shape[0]
    return jnp.moveaxis(pieces, 0, dim).reshape(lengths)


def gather_in_order(x, axes, order):
    pieces = x
    for k in order:
        pieces = lax.all_gather(pieces, axes[k])
    done = order[::-1]
    back = [done.index(k) for k in range(len(axes))]
    pieces = pieces.transpose(*back, *range(len(axes), pieces.ndim))
    return pieces.reshape(-1, *x.shape)


def gather_axes(x, axes, order, dim):
    return joined_along(gather_in_order(x, axes, order), dim)


def copy_for_each(x, axis):
    copies = jnp.broadcast_to(x, (lax.axis_size(axis), *x.shape))
    return lax.all_to_all(copies, axis, split_axis=0, concat_axis=0, tiled=True)


def of_everyone(x, axis):
    everything = copy_for_each(x, axis)
    return jnp.sum(everything, axis=0)


def rope_tables(places_int, head_width):
    half_width = head_width // 2
    exponent = jnp.arange(half_width, dtype=jnp.float32) * (-2.0 / head_width)
    inverse = jnp.power(rope_base, exponent)
    places = places_int.astype(jnp.float32)
    angles = places[:, :, None] * inverse[None, None, :]
    return (jnp.cos(angles)[:, :, None, :], jnp.sin(angles)[:, :, None, :])


def rotate(values, cosine, sine_part):
    half_width = values.shape[-1] // 2
    leading = values[..., :half_width]
    trailing = values[..., half_width:]
    return jnp.concatenate(
        [leading * cosine - trailing * sine_part, trailing * cosine + leading * sine_part], axis=-1
    )


def rotate_back(values, cosine, sine_part):
    half_width = values.shape[-1] // 2
    leading = values[..., :half_width]
    trailing = values[..., half_width:]
    return jnp.concatenate(
        [leading * cosine + trailing * sine_part, trailing * cosine - leading * sine_part], axis=-1
    )


def norm_back(grad_hat, normed, scale):
    return scale * (grad_hat - normed * jnp.mean(grad_hat * normed, axis=-1, keepdims=True))


def head_normalize(raw_proj, slot_count, length, heads):
    shaped = raw_proj.reshape(slot_count, length, heads, HD)
    scale = lax.rsqrt(jnp.mean(shaped * shaped, axis=-1, keepdims=True) + norm_eps)
    return (shaped * scale, scale)


def head_back(grad_rot, normed, scale, gain, cosine, sine_part):
    grad_gained = rotate_back(grad_rot, cosine, sine_part)
    gain_term = jnp.sum(grad_gained * normed, axis=(0, 1, 2))
    grad_raw = norm_back(grad_gained * gain, normed, scale)
    return (
        grad_raw.reshape(grad_raw.shape[0] * grad_raw.shape[1], -1).astype(jnp.bfloat16),
        gain_term,
    )


def contract_last(left, right):
    return lax.dot_general(
        left, right, (((1,), (1,)), ((), ())), preferred_element_type=jnp.float32
    )


def slot_layout(row_block, matrix_slot, slot_ids, widths):
    layout = jnp.zeros((slot_ids.shape[0], row_block.shape[0], FF), jnp.float32)
    offset = 0
    for number in range(7):
        column_piece = row_block[:, offset : offset + widths[number]]
        offset = offset + widths[number]
        padded = jnp.pad(column_piece, ((0, 0), (0, FF - widths[number])))
        matches = (slot_ids == matrix_slot[number])[:, None, None]
        layout = layout + jnp.where(matches, padded[None], 0.0)
    return layout


def shards(
    hidden_in,
    out_grad,
    seq_owner,
    token_place,
    matrix_slot,
    weight_slots,
    momentum_slots,
    gains,
    gain_momentum,
):
    slot_count = hidden_in.shape[0]
    length = hidden_in.shape[1]
    tok_count = slot_count * length
    group_here = lax.axis_index("group")
    replica = lax.axis_index(DP) * lax.axis_size("group") + group_here
    live_count = jnp.sum((seq_owner == replica).astype(jnp.int32))
    live_slot = (jnp.arange(slot_count, dtype=jnp.int32) < live_count).astype(jnp.float32)
    live_token = jnp.repeat(live_slot, length)[:, None]
    weight_low = weight_slots.astype(jnp.bfloat16)
    partial_set = lax.all_gather(weight_low, "group", axis=0, tiled=True)
    all_slots = gather_axes(partial_set, (("dp_0", "dp_1"), "dp_2"), (0, 1), 1)
    widths = (HEADS * HD, KV * HD, KV * HD, HEADS * HD, FF, FF, FF)
    chosen = []
    for number in range(7):
        whole_slot = lax.dynamic_index_in_dim(all_slots, matrix_slot[number], 0, keepdims=False)
        chosen.append(whole_slot[:, : widths[number]])
    w_query, w_key, w_value, w_output, w_gate, w_up, w_down = chosen
    tokens = hidden_in.astype(jnp.float32).reshape(tok_count, D)
    gain_one = gains[:D]
    gain_two = gains[D : 2 * D]
    gain_query = gains[2 * D : 2 * D + HD]
    gain_key = gains[2 * D + HD :]
    cosine, sine_part = rope_tables(token_place, HD)
    scale_one = lax.rsqrt(jnp.mean(tokens * tokens, axis=-1, keepdims=True) + norm_eps)
    normed_one = tokens * scale_one
    input_one = (normed_one * gain_one).astype(jnp.bfloat16)
    query_raw = jnp.dot(input_one, w_query, preferred_element_type=jnp.float32)
    key_raw = jnp.dot(input_one, w_key, preferred_element_type=jnp.float32)
    value_low = jnp.dot(input_one, w_value, preferred_element_type=jnp.float32).astype(jnp.bfloat16)
    query_hat, query_scale = head_normalize(query_raw, slot_count, length, HEADS)
    key_hat, key_scale = head_normalize(key_raw, slot_count, length, KV)
    query_low = rotate(query_hat * gain_query, cosine, sine_part).astype(jnp.bfloat16)
    key_low = rotate(key_hat * gain_key, cosine, sine_part).astype(jnp.bfloat16)
    query_group = query_low.reshape(slot_count, length, KV, HEADS // KV, HD)
    value_heads = value_low.reshape(slot_count, length, KV, HD)
    causal = jnp.arange(length)[:, None] >= jnp.arange(length)[None, :]
    score_scale = HD ** (-0.5)

    def scores_of(query_part, key_part):
        raw_scores = (
            jnp.einsum(
                "bikgw,bjkw->bkgij", query_part, key_part, preferred_element_type=jnp.float32
            )
            * score_scale
        )
        return jnp.where(causal, raw_scores, masked_score)

    scores = scores_of(query_group, key_low)
    row_top = jnp.max(scores, axis=-1, keepdims=True)
    exponent_terms = jnp.exp(scores - row_top)
    row_total = jnp.sum(exponent_terms, axis=-1, keepdims=True)
    log_total = row_top + jnp.log(row_total)
    probs_low = (exponent_terms / row_total).astype(jnp.bfloat16)
    attended = jnp.einsum(
        "bkgij,bjkw->bikgw", probs_low, value_heads, preferred_element_type=jnp.float32
    )
    attn_low = attended.reshape(tok_count, HEADS * HD).astype(jnp.bfloat16)
    residual = tokens + contract_last(attn_low, w_output)
    scale_two = lax.rsqrt(jnp.mean(residual * residual, axis=-1, keepdims=True) + norm_eps)
    normed_two = residual * scale_two
    input_two = (normed_two * gain_two).astype(jnp.bfloat16)
    gate_proj = jnp.dot(input_two, w_gate, preferred_element_type=jnp.float32)
    up_proj = jnp.dot(input_two, w_up, preferred_element_type=jnp.float32)
    sigmoid_gate = jax.nn.sigmoid(gate_proj)
    swish_gate = gate_proj * sigmoid_gate
    act_low = (swish_gate * up_proj).astype(jnp.bfloat16)
    result = (residual + contract_last(act_low, w_down)) * live_token
    hidden_out = result.astype(jnp.bfloat16).reshape(slot_count, length, D)
    grad_out = out_grad.astype(jnp.float32).reshape(tok_count, D) * live_token
    grad_low = grad_out.astype(jnp.bfloat16)
    grad_act = jnp.dot(grad_low, w_down, preferred_element_type=jnp.float32)
    swish_slope = sigmoid_gate * (1.0 + gate_proj * (1.0 - sigmoid_gate))
    grad_gate = (grad_act * up_proj * swish_slope).astype(jnp.bfloat16)
    grad_up = (grad_act * swish_gate).astype(jnp.bfloat16)
    grad_two = contract_last(grad_gate, w_gate) + contract_last(grad_up, w_up)
    gain_two_grad = jnp.sum(grad_two * normed_two, axis=0)
    grad_residual = grad_out + norm_back(grad_two * gain_two, normed_two, scale_two)
    branch_low = grad_residual.astype(jnp.bfloat16)
    grad_attn = jnp.dot(branch_low, w_output, preferred_element_type=jnp.float32)
    grad_attn_low = grad_attn.astype(jnp.bfloat16).reshape(slot_count, length, KV, HEADS // KV, HD)
    probs = jnp.exp(scores_of(query_group, key_low) - log_total)
    grad_value = jnp.einsum(
        "bkgij,bikgw->bjkw", probs_low, grad_attn_low, preferred_element_type=jnp.float32
    )
    grad_value_low = grad_value.reshape(tok_count, KV * HD).astype(jnp.bfloat16)
    grad_probs = jnp.einsum(
        "bikgw,bjkw->bkgij", grad_attn_low, value_heads, preferred_element_type=jnp.float32
    )
    grad_scores = (
        probs * (grad_probs - jnp.sum(probs * grad_probs, axis=-1, keepdims=True))
    ).astype(jnp.bfloat16)
    grad_query_rot = (
        jnp.einsum("bkgij,bjkw->bikgw", grad_scores, key_low, preferred_element_type=jnp.float32)
        * score_scale
    )
    grad_key_rot = (
        jnp.einsum(
            "bkgij,bikgw->bjkw", grad_scores, query_group, preferred_element_type=jnp.float32
        )
        * score_scale
    )
    grad_query_low, gain_query_grad = head_back(
        grad_query_rot.reshape(slot_count, length, HEADS, HD),
        query_hat,
        query_scale,
        gain_query,
        cosine,
        sine_part,
    )
    grad_key_low, gain_key_grad = head_back(
        grad_key_rot, key_hat, key_scale, gain_key, cosine, sine_part
    )
    grad_one = (
        contract_last(grad_query_low, w_query)
        + contract_last(grad_key_low, w_key)
        + contract_last(grad_value_low, w_value)
    )
    gain_one_grad = jnp.sum(grad_one * normed_one, axis=0)
    in_grad = (grad_residual + norm_back(grad_one * gain_one, normed_one, scale_one)).reshape(
        slot_count, length, D
    )
    pairs = (
        (input_one, grad_query_low),
        (input_one, grad_key_low),
        (input_one, grad_value_low),
        (branch_low, attn_low),
        (input_two, grad_gate),
        (input_two, grad_up),
        (grad_low, act_low),
    )
    own_ids = group_here * 2 + jnp.arange(2, dtype=jnp.int32)
    blocks_out = []
    for left_side, right_side in pairs:
        product = lax.dot_general(
            left_side, right_side, (((0,), (0,)), ((), ())), preferred_element_type=jnp.float32
        )
        blocks_out.append(product.astype(jnp.bfloat16).astype(jnp.float32))
    partial_rows = lax.psum_scatter(
        jnp.concatenate(blocks_out, axis=1).astype(jnp.bfloat16),
        DP,
        scatter_dimension=0,
        tiled=True,
    ).astype(jnp.float32)
    every_slot = jnp.arange(2 * lax.axis_size("group"), dtype=jnp.int32)
    routed = slot_layout(partial_rows, matrix_slot, every_slot, widths)
    weight_grad = lax.psum_scatter(
        routed.astype(jnp.bfloat16), "group", scatter_dimension=0, tiled=True
    ).astype(jnp.float32)
    gain_term = (
        jnp.concatenate([gain_one_grad, gain_two_grad, gain_query_grad, gain_key_grad])
        .astype(jnp.bfloat16)
        .astype(jnp.float32)
    )
    gain_grad = lax.psum(gain_term, DP_GROUP)
    own_width = jnp.zeros((2,), jnp.int32)
    for number in range(7):
        own_width = own_width + jnp.where(own_ids == matrix_slot[number], widths[number], 0).astype(
            jnp.int32
        )
    column_mask = (jnp.arange(FF, dtype=jnp.int32)[None, :] < own_width[:, None]).astype(
        jnp.float32
    )[:, None, :]
    momentum_new = column_mask * (momentum_keep * momentum_slots + weight_grad)
    direction = weight_grad + momentum_keep * momentum_new
    squares = of_everyone(jnp.sum(direction * direction, axis=(1, 2)), DP)
    iterate = (direction / (jnp.sqrt(squares)[:, None, None] + frob_eps)).astype(jnp.bfloat16)
    for sweep_index in range(NS_ITERS):
        full_rows = lax.all_gather(iterate, DP, axis=1, tiled=True)
        gram_low = jnp.einsum(
            "sin,sjn->sij", iterate, full_rows, preferred_element_type=jnp.float32
        ).astype(jnp.bfloat16)
        full_gram = lax.all_gather(gram_low, DP, axis=1, tiled=True)
        gram_square = jnp.einsum(
            "sij,sjk->sik", gram_low, full_gram, preferred_element_type=jnp.float32
        )
        poly_low = (coef_square * gram_low.astype(jnp.float32) + coef_quartic * gram_square).astype(
            jnp.bfloat16
        )
        mixed = jnp.einsum("sij,sjn->sin", poly_low, full_rows, preferred_element_type=jnp.float32)
        iterate = (coef_linear * iterate.astype(jnp.float32) + mixed).astype(jnp.bfloat16)
    update_scale = 0.2 * jnp.sqrt(jnp.maximum(own_width, D).astype(jnp.float32))
    weight_new = column_mask * (
        weight_slots * (1.0 - learn_rate * weight_decay)
        - learn_rate * update_scale[:, None, None] * iterate.astype(jnp.float32)
    )
    gain_momentum_new = momentum_keep * gain_momentum + gain_grad
    gain_step = gain_grad + momentum_keep * gain_momentum_new
    bounds = (0, D, 2 * D, 2 * D + HD, 2 * D + 2 * HD)
    scaled_parts = []
    for number in range(4):
        segment = gain_step[bounds[number] : bounds[number + 1]]
        scaled_parts.append(segment * lax.rsqrt(jnp.mean(segment * segment) + norm_eps))
    gain_new = gains - gain_rate * jnp.concatenate(scaled_parts)
    return (
        hidden_out,
        in_grad,
        weight_grad,
        momentum_new,
        weight_new,
        gain_grad,
        gain_momentum_new,
        gain_new,
    )


def solution(mesh):
    finer = Mesh(
        mesh.devices.reshape(4, 4, 2, mesh.shape["group"]), ("dp_0", "dp_1", "dp_2", "group")
    )
    in_specs = (
        P(DP_GROUP, None, None),
        P(DP_GROUP, None, None),
        P(),
        P(DP_GROUP, None),
        P(),
        P("group", DP, None),
        P("group", DP, None),
        P(),
        P(),
    )
    out_specs = (
        P(DP_GROUP, None, None),
        P(DP_GROUP, None, None),
        P("group", DP, None),
        P("group", DP, None),
        P("group", DP, None),
        P(),
        P(),
        P(),
    )
    return jax.shard_map(
        shards, mesh=finer, in_specs=in_specs, out_specs=out_specs, check_vma=False
    )
```

profile of v0, /device:TPU:1, one launch (start us, length us, event | category | flops | bytes accessed | tf_op | source)
XLA Modules:
  0.0 1390.5 jit_solution(15375148760091633531)
XLA Ops:
  9.2 30.8 %all-gather.16.cloned.1.call-done = bf16[8,32,3072]{2,1,0:T(8,128)(2,1)} async-done(((bf16[2,32,3072]{2,1,0:T(8,128)(2,1)}), bf16[8,32,3072]{2,1,0:T(8,128)(2,1)}) %all-gather.16.cloned.1.call-update) | async-done | bytes 1572880 | tf_op jit(solution)/shard_map/all_gather | solution.py:145
  40.0 156.5 %all-gather.38.cloned.1.call-done = bf16[128,32,3072]{2,1,0:T(8,128)(2,1)} async-done(((bf16[8,32,3072]{2,1,0:T(8,128)(2,1)}), bf16[128,32,3072]{2,1,0:T(8,128)(2,1)}) %all-gather.38.cloned.1.call-update) | async-done | bytes 25165840 | tf_op jit(solution)/shard_map/all_gather | solution.py:39
  217.3 56.9 %all-gather.40.cloned.1.call-done = bf16[32,8,32,3072]{3,2,1,0:T(8,128)(2,1)} async-done(((bf16[16,8,32,3072]{3,2,1,0:T(8,128)(2,1)}), bf16[32,8,32,3072]{3,2,1,0:T(8,128)(2,1)}) %all-gather.40.cloned.1.call-update) | async-done | bytes 50331664 | tf_op jit(solution)/shard_map/all_gather | solution.py:39
  274.2 33.6 %copy.116 = bf16[16,2,8,32,3072]{4,3,2,1,0:T(8,128)(2,1)} copy(bf16[16,2,8,32,3072]{4,3,2,0,1:T(8,128)(2,1)} %bitcast.235) | data formatting | bytes 100663296 | tf_op jit(solution)/shard_map/transpose | solution.py:42
  307.7 33.5 %copy.117 = bf16[8,32,32,3072]{3,2,1,0:T(8,128)(2,1)} copy(bf16[8,32,32,3072]{3,2,0,1:T(8,128)(2,1)} %bitcast.227) | data formatting | bytes 100663296 | tf_op jit(solution)/shard_map/transpose | solution.py:33
  341.3 14.5 %dynamic-slice_bitcast_fusion = (bf16[1024,3072]{1,0:T(8,128)(2,1)}, bf16[1024,3072]{1,0:T(8,128)(2,1)}, bf16[1024,3072]{1,0:T(8,128)(2,1)S(1)}, bf16[1024,3072]{1,0:T(8,128)(2,1)S(1)}) fusion(bf16[8,1024,3072]{2,1,0:T(8,128)(2,1)} %bitcast.228, s32[]{:T(128)S(6)} %select_n.131, s32[]{:T(128)S(6)} %select_n.129, s32[]{:T(128)S(6)} %select_n.128, ...), kind=kLoop, calls=%fused_computation.15 | loop fusion | bytes 50331664 | tf_op jit(solution)/shard_map/jit(dynamic_index_in_dim)/squeeze | solution.py:150
  371.5 6.5 copy.119
  412.3 7.3 multiply_convert_fusion.1
  419.6 5.7 fusion.4
  503.8 155.9 %reduce-scatter.3.cloned.1.call-done = bf16[32,15360]{1,0:T(8,128)(2,1)} async-done(((bf16[1024,15360]{1,0:T(8,128)(2,1)}), bf16[32,15360]{1,0:T(8,128)(2,1)}) %reduce-scatter.3.cloned.1.call-update) | async-done | bytes 983056 | tf_op jit(solution)/shard_map/reduce_scatter | solution.py:273
  670.0 19.8 %reduce-scatter.5.cloned.1.call-done = bf16[2,32,3072]{2,1,0:T(8,128)(2,1)} async-done(((bf16[8,32,3072]{2,1,0:T(8,128)(2,1)}), bf16[2,32,3072]{2,1,0:T(8,128)(2,1)}) %reduce-scatter.5.cloned.1.call-update) | async-done | bytes 393232 | tf_op jit(solution)/shard_map/reduce_scatter | solution.py:281
  691.3 15.5 %all_to_all.6 = f32[32,1,2]{2,1,0:T(1,128)S(1)} all-to-all(f32[32,1,2]{2,1,0:T(1,128)S(1)} %broadcast_in_dim.192), channel_id=1, replica_groups=mesh['dp_0'=4,'dp_1'=4,'dp_2'=2,'group'=4] {'dp_0','dp_1','dp_2'}, dimensions={0} | all-to-all | bytes 512 | tf_op jit(solution)/shard_map/all_to_all | solution.py:52
  708.0 59.3 %all-gather.18.cloned.1.call-done = bf16[2,1024,3072]{2,1,0:T(8,128)(2,1)} async-done(((bf16[2,32,3072]{2,1,0:T(8,128)(2,1)}), bf16[2,1024,3072]{2,1,0:T(8,128)(2,1)}) %all-gather.18.cloned.1.call-update) | async-done | bytes 12582928 | tf_op jit(solution)/shard_map/all_gather | solution.py:303
  767.3 9.2 convolution_convert_fusion.7
  776.5 46.0 %all-gather.20.cloned.1.call-done = bf16[2,1024,1024]{2,1,0:T(8,128)(2,1)} async-done(((bf16[2,32,1024]{2,1,0:T(8,128)(2,1)}), bf16[2,1024,1024]{2,1,0:T(8,128)(2,1)}) %all-gather.20.cloned.1.call-update) | async-done | bytes 4194320 | tf_op jit(solution)/shard_map/all_gather | solution.py:307
  822.5 9.7 fusion.24
  832.3 62.3 %all-gather.22.cloned.1.call-done = bf16[2,1024,3072]{2,1,0:T(8,128)(2,1)} async-done(((bf16[2,32,3072]{2,1,0:T(8,128)(2,1)}), bf16[2,1024,3072]{2,1,0:T(8,128)(2,1)}) %all-gather.22.cloned.1.call-update) | async-done | bytes 12582928 | tf_op jit(solution)/shard_map/all_gather | solution.py:303
  894.6 9.2 convolution_convert_fusion.6
  903.9 46.0 %all-gather.24.cloned.1.call-done = bf16[2,1024,1024]{2,1,0:T(8,128)(2,1)} async-done(((bf16[2,32,1024]{2,1,0:T(8,128)(2,1)}), bf16[2,1024,1024]{2,1,0:T(8,128)(2,1)}) %all-gather.24.cloned.1.call-update) | async-done | bytes 4194320 | tf_op jit(solution)/shard_map/all_gather | solution.py:307
  949.9 9.7 fusion.25
  959.9 62.1 %all-gather.26.cloned.1.call-done = bf16[2,1024,3072]{2,1,0:T(8,128)(2,1)} async-done(((bf16[2,32,3072]{2,1,0:T(8,128)(2,1)}), bf16[2,1024,3072]{2,1,0:T(8,128)(2,1)}) %all-gather.26.cloned.1.call-update) | async-done | bytes 12582928 | tf_op jit(solution)/shard_map/all_gather | solution.py:303
  1022.0 9.2 convolution_convert_fusion.5
  1031.2 46.0 %all-gather.28.cloned.1.call-done = bf16[2,1024,1024]{2,1,0:T(8,128)(2,1)} async-done(((bf16[2,32,1024]{2,1,0:T(8,128)(2,1)}), bf16[2,1024,1024]{2,1,0:T(8,128)(2,1)}) %all-gather.28.cloned.1.call-update) | async-done | bytes 4194320 | tf_op jit(solution)/shard_map/all_gather | solution.py:307
  1077.2 9.7 fusion.26
  1087.0 62.3 %all-gather.30.cloned.1.call-done = bf16[2,1024,3072]{2,1,0:T(8,128)(2,1)} async-done(((bf16[2,32,3072]{2,1,0:T(8,128)(2,1)}), bf16[2,1024,3072]{2,1,0:T(8,128)(2,1)}) %all-gather.30.cloned.1.call-update) | async-done | bytes 12582928 | tf_op jit(solution)/shard_map/all_gather | solution.py:303
  1149.3 9.2 convolution_convert_fusion.4
  1158.6 46.0 %all-gather.32.cloned.1.call-done = bf16[2,1024,1024]{2,1,0:T(8,128)(2,1)} async-done(((bf16[2,32,1024]{2,1,0:T(8,128)(2,1)}), bf16[2,1024,1024]{2,1,0:T(8,128)(2,1)}) %all-gather.32.cloned.1.call-update) | async-done | bytes 4194320 | tf_op jit(solution)/shard_map/all_gather | solution.py:307
  1204.6 9.7 fusion.27
  1214.6 62.1 %all-gather.34.cloned.1.call-done = bf16[2,1024,3072]{2,1,0:T(8,128)(2,1)} async-done(((bf16[2,32,3072]{2,1,0:T(8,128)(2,1)}), bf16[2,1024,3072]{2,1,0:T(8,128)(2,1)}) %all-gather.34.cloned.1.call-update) | async-done | bytes 12582928 | tf_op jit(solution)/shard_map/all_gather | solution.py:303
  1276.7 9.2 convolution_convert_fusion.3
  1295.6 64.9 %psum.7 = f32[2304]{0:T(1024)S(1)} all-reduce(f32[2304]{0:T(1024)S(1)} %maximum_convert_fusion), channel_id=1, replica_groups=mesh['dp_0'=4,'dp_1'=4,'dp_2'=2,'group'=4] {'dp_0','dp_1','dp_2','group'}, use_global_device_ids=true, to_apply=%region_20.21 | all-reduce | flops 2304 | bytes 18432 | tf_op jit(solution)/shard_map/psum | solution.py:289
  1373.8 9.8 fusion.32
  (298 shorter events, 171.5 us)
Async XLA Ops:
  7.2 32.8 %all-gather.16.cloned.1.call-start = ((), (), s32[]{:S(2)}) async-start(), calls=%async_computation.3 | async-start | bytes 1966080 | tf_op jit(solution)/shard_map/all_gather | solution.py:145
  9.2 187.4 %all-gather.38.cloned.1.call-start = ((), (), s32[]{:S(2)}) async-start(), calls=%async_computation.16 | async-start | bytes 26738688 | tf_op jit(solution)/shard_map/all_gather | solution.py:39
  40.0 234.2 %all-gather.40.cloned.1.call-start = ((), (), s32[]{:S(2)}) async-start(), calls=%async_computation.17 | async-start | bytes 75497472 | tf_op jit(solution)/shard_map/all_gather | solution.py:39
  196.6 18.6 %copy-start.31 = (bf16[2,128,1024]{2,1,0:T(8,128)(2,1)S(1)}, bf16[2,128,1024]{2,1,0:T(8,128)(2,1)}, u32[]{:S(2)}) copy-start(bf16[2,128,1024]{2,1,0:T(8,128)(2,1)} %param.10) | copy-start | bytes 1572868
  196.6 463.1 %reduce-scatter.3.cloned.1.call-start = ((), (), s32[]{:S(2)}) async-start(), calls=%async_computation.4 | async-start | bytes 32440320 | tf_op jit(solution)/shard_map/reduce_scatter | solution.py:273
  213.6 94.1 %copy-start.57 = (f32[256]{0:T(256)}, f32[256]{0:T(256)S(1)}, u32[]{:S(2)}) copy-start(f32[256]{0:T(256)S(1)} %get-tuple-element.60) | copy-start | bytes 3076
  214.2 167.3 %copy-start.61 = (f32[128]{0:T(128)}, f32[128]{0:T(128)S(1)}, u32[]{:S(2)}) copy-start(f32[128]{0:T(128)S(1)} %get-tuple-element.56) | copy-start | bytes 1540
  214.8 92.9 %copy-start.49 = (f32[1024]{0:T(1024)}, f32[1024]{0:T(1024)S(1)}, u32[]{:S(2)}) copy-start(f32[1024]{0:T(1024)S(1)} %get-tuple-element.54) | copy-start | bytes 12292
  402.4 28.7 %copy-start.23 = (f32[256,1024]{1,0:T(8,128)}, f32[256,1024]{1,0:T(8,128)S(1)}, u32[]{:S(2)}) copy-start(f32[256,1024]{1,0:T(8,128)S(1)} %get-tuple-element.75) | copy-start | bytes 3145732
  499.4 162.5 %copy-start.63 = (pred[3072]{0:T(1024)(128)(4,1)S(1)}, pred[3072]{0:T(1024)(128)(4,1)}, u32[]{:S(2)}) copy-start(pred[3072]{0:T(1024)(128)(4,1)} %constant.97.clone.1) | copy-start | bytes 9220
  499.4 190.4 %reduce-scatter.5.cloned.1.call-start = ((), (), s32[]{:S(2)}) async-start(), calls=%async_computation.5 | async-start | bytes 1966080 | tf_op jit(solution)/shard_map/reduce_scatter | solution.py:281
  665.5 101.7 %all-gather.18.cloned.1.call-start = ((), (), s32[]{:S(2)}) async-start(), calls=%async_computation.6 | async-start | bytes 12976128 | tf_op jit(solution)/shard_map/all_gather | solution.py:303
  691.3 85.2 %copy-start.28 = (f32[2,32,3072]{2,1,0:T(8,128)}, f32[2,32,3072]{2,1,0:T(8,128)S(1)}, u32[]{:S(2)}) copy-start(f32[2,32,3072]{2,1,0:T(8,128)S(1)} %get-tuple-element.25) | copy-start | bytes 2359300
  691.3 85.2 %copy-start.29 = (f32[2,32,3072]{2,1,0:T(8,128)}, f32[2,32,3072]{2,1,0:T(8,128)S(1)}, u32[]{:S(2)}) copy-start(f32[2,32,3072]{2,1,0:T(8,128)S(1)} %get-tuple-element.26) | copy-start | bytes 2359300
  707.8 114.8 %copy-start.7 = (bf16[2,32,3072]{2,1,0:T(8,128)(2,1)S(1)}, bf16[2,32,3072]{2,1,0:T(8,128)(2,1)}, u32[]{:S(2)}) copy-start(bf16[2,32,3072]{2,1,0:T(8,128)(2,1)} %divide_convert_fusion.1) | copy-start | bytes 1179652
  707.8 114.8 %all-gather.20.cloned.1.call-start = ((), (), s32[]{:S(2)}) async-start(), calls=%async_computation.7 | async-start | bytes 4325376 | tf_op jit(solution)/shard_map/all_gather | solution.py:307
  776.5 118.1 %all-gather.22.cloned.1.call-start = ((), (), s32[]{:S(2)}) async-start(), calls=%async_computation.8 | async-start | bytes 12976128 | tf_op jit(solution)/shard_map/all_gather | solution.py:303
  832.2 117.6 %copy-start.1 = (bf16[2,32,3072]{2,1,0:T(8,128)(2,1)S(1)}, bf16[2,32,3072]{2,1,0:T(8,128)(2,1)}, u32[]{:S(2)}) copy-start(bf16[2,32,3072]{2,1,0:T(8,128)(2,1)} %fusion.24) | copy-start | bytes 1179652
  832.3 117.6 %all-gather.24.cloned.1.call-start = ((), (), s32[]{:S(2)}) async-start(), calls=%async_computation.9 | async-start | bytes 4325376 | tf_op jit(solution)/shard_map/all_gather | solution.py:307
  903.9 118.1 %all-gather.26.cloned.1.call-start = ((), (), s32[]{:S(2)}) async-start(), calls=%async_computation.10 | async-start | bytes 12976128 | tf_op jit(solution)/shard_map/all_gather | solution.py:303
  959.6 117.6 %copy-start.2 = (bf16[2,32,3072]{2,1,0:T(8,128)(2,1)S(1)}, bf16[2,32,3072]{2,1,0:T(8,128)(2,1)}, u32[]{:S(2)}) copy-start(bf16[2,32,3072]{2,1,0:T(8,128)(2,1)} %fusion.25) | copy-start | bytes 1179652
  959.6 117.6 %all-gather.28.cloned.1.call-start = ((), (), s32[]{:S(2)}) async-start(), calls=%async_computation.11 | async-start | bytes 4325376 | tf_op jit(solution)/shard_map/all_gather | solution.py:307
  1031.2 118.1 %all-gather.30.cloned.1.call-start = ((), (), s32[]{:S(2)}) async-start(), calls=%async_computation.12 | async-start | bytes 12976128 | tf_op jit(solution)/shard_map/all_gather | solution.py:303
  1086.9 117.6 %copy-start.3 = (bf16[2,32,3072]{2,1,0:T(8,128)(2,1)S(1)}, bf16[2,32,3072]{2,1,0:T(8,128)(2,1)}, u32[]{:S(2)}) copy-start(bf16[2,32,3072]{2,1,0:T(8,128)(2,1)} %fusion.26) | copy-start | bytes 1179652
  1087.0 117.6 %all-gather.32.cloned.1.call-start = ((), (), s32[]{:S(2)}) async-start(), calls=%async_computation.13 | async-start | bytes 4325376 | tf_op jit(solution)/shard_map/all_gather | solution.py:307
  1158.5 118.1 %all-gather.34.cloned.1.call-start = ((), (), s32[]{:S(2)}) async-start(), calls=%async_computation.14 | async-start | bytes 12976128 | tf_op jit(solution)/shard_map/all_gather | solution.py:303
  1214.3 71.6 %copy-start.37 = (bf16[2,128,16,128]{3,2,1,0:T(8,128)(2,1)S(1)}, bf16[2,128,16,128]{3,2,1,0:T(8,128)(2,1)}, u32[]{:S(2)}) copy-start(bf16[2,128,16,128]{3,2,1,0:T(8,128)(2,1)} %copy.129) | copy-start | bytes 3145732
  1214.3 159.4 %all-gather.36.cloned.1.call-start = ((), (), s32[]{:S(2)}) async-start(), calls=%async_computation.15 | async-start | bytes 4325376 | tf_op jit(solution)/shard_map/all_gather | solution.py:307
  1292.0 68.4 %copy-start.56 = (f32[2304]{0:T(1024)S(1)}, f32[2304]{0:T(1024)}, u32[]{:S(2)}) copy-start(f32[2304]{0:T(1024)} %param.17) | copy-start | bytes 27652
  1292.0 73.0 %copy-start.53 = (f32[2304]{0:T(1024)S(1)}, f32[2304]{0:T(1024)}, u32[]{:S(2)}) copy-start(f32[2304]{0:T(1024)} %param.16) | copy-start | bytes 27652
  1295.5 72.7 %copy-start.24 = (f32[256,1024]{1,0:T(8,128)S(1)}, f32[256,1024]{1,0:T(8,128)}, u32[]{:S(2)}) copy-start(f32[256,1024]{1,0:T(8,128)} %copy-done.23) | copy-start | bytes 3145732
  1295.5 72.7 %copy-start.68 = (f32[256]{0:T(256)S(1)}, f32[256]{0:T(256)}, u32[]{:S(2)}) copy-start(f32[256]{0:T(256)} %broadcast_bitcast_fusion) | copy-start | bytes 3076
  (62 other events, 286.9 us)
Sparse Core Ops, SparseCore 0:
  10.2 29.6 all-gather.15
  42.1 154.3 all-gather.37
  198.2 75.9 all-gather.39
  499.5 160.1 reduce-scatter.2
  665.7 24.0 reduce-scatter.4
  707.9 59.3 all-gather.17
  776.6 45.8 all-gather.19
  832.4 62.2 all-gather.21
  904.0 45.8 all-gather.23
  959.7 62.2 all-gather.25
  1031.3 45.8 all-gather.27
  1087.1 62.2 all-gather.29
  1158.7 45.8 all-gather.31
  1214.4 62.2 all-gather.33
  1286.0 46.1 all-gather.35
where the time goes:
time: 1400 us; the launch traced here: 1390 us
  waiting for transfers between devices  912 us (65%)
  matrix products  186 us (13%)
  local copies, waits for them, and re-layouts  142 us (10%)
  blocking collectives  80.3 us (6%)
  other arithmetic  37.8 us (3%)
  between operations  31.2 us (2%)
    all_gather x5, waiting for transfers between devices, shards(): full_rows = lax.all_gather(iterate, DP, axis=1, tiled=True)  308 us
    all_gather x2, waiting for transfers between devices, gather_in_order(): pieces = lax.all_gather(pieces, axes[k])  213 us
    all_gather x5, waiting for transfers between devices, shards(): full_gram = lax.all_gather(gram_low, DP, axis=1, tiled=True)  184 us
    reduce_scatter x1, waiting for transfers between devices, shards(): lax.psum_scatter(jnp.concatenate(blocks_out, axis=1).astype(jnp.bfloat16)...  156 us
    psum x1, blocking collectives, shards(): gain_grad = lax.psum(gain_term, DP_GROUP)  64.9 us
    dot_general x5, matrix products, shards(): jnp.einsum('sij,sjn->sin', poly_low, full_rows, preferred_element_type=jn...  48.6 us
    dot_general x5, matrix products, shards(): jnp.einsum('sin,sjn->sij', iterate, full_rows, preferred_element_type=jnp...  46 us
    transpose x1, local copies, waits for them, and re-layouts, gather_in_order(): pieces = pieces.transpose(*back, *range(len(axes), pieces.ndim))  33.6 us
  transfers between devices with their start and end apart: 15, of which 14 were waited for; matrix products, arithmetic and copies ran while one was open for 3% of the time, Pallas kernels for 0%

commit v1 on v0

v1 whole, which is shorter than its diff:
```python
import functools

import jax
import jax.numpy as jnp
from jax import lax
from jax.experimental import pallas as pl
from jax.experimental.pallas import tpu as pltpu
from jax.sharding import Mesh
from jax.sharding import PartitionSpec as P

D = 1024
HEADS = 16
KV = 8
HD = 128
FF = 3072
SEQ = 128
NS_ITERS = 5
WIDTHS = (HEADS * HD, KV * HD, KV * HD, HEADS * HD, FF, FF, FF)
DP_GROUP = ("dp_0", "dp_1", "dp_2", "group")
LOW = jnp.bfloat16
F32 = jnp.float32

norm_eps = 1e-06
frob_eps = 1e-07
rope_base = 1000000.0
coef_linear = 3.4445
coef_square = -4.775
coef_quartic = 2.0315
momentum_keep = 0.95
learn_rate = 0.15
weight_decay = 0.1
gain_rate = 0.5
masked_score = -1e30
score_scale = HD ** (-0.5)

NEAR = ((0, 1), (1, 0), (2, 3), (3, 2))
FAR = ((0, 3), (3, 0), (1, 2), (2, 1))
LINKS = (("dp_0", NEAR), ("dp_1", NEAR), ("dp_0", FAR), ("dp_1", FAR))
MASKS = (0, 3, 1, 2)


def place_of(mask):
    return jnp.where(mask == 0, 0, jnp.where(mask == 3, 1, mask + 1))


def swap(x):
    return lax.ppermute(x, "dp_2", ((0, 1), (1, 0)))


def together(arrays):
    return list(lax.optimization_barrier(tuple(arrays)))


def gather_steps(quarters, step):
    fresh = []
    for i in range(4):
        axis, pairs = LINKS[(step + i) % 4]
        fresh.append(lax.ppermute(quarters[i], axis, pairs))
    return [
        jnp.concatenate([quarters[i], fresh[i]], axis=(step + i) % 4) for i in range(4)
    ]


def gather_quarters(quarters):
    rows = quarters[0].shape[0]
    held = [q.reshape(1, 1, 1, 1, rows, q.shape[1]) for q in quarters]
    for step in range(4):
        held = gather_steps(held, step)
        if step < 3:
            held = together(held)
    return [q.reshape(16 * rows, q.shape[-1]) for q in held]


def scatter_quarters(quarters):
    rows = quarters[0].shape[0] // 16
    held = [q.reshape(2, 2, 2, 2, rows, q.shape[1]) for q in quarters]
    for step in range(4):
        sent = [lax.slice_in_dim(held[i], 1, 2, axis=(step + i) % 4) for i in range(4)]
        kept = [lax.slice_in_dim(held[i], 0, 1, axis=(step + i) % 4) for i in range(4)]
        got = []
        for i in range(4):
            axis, pairs = LINKS[(step + i) % 4]
            got.append(lax.ppermute(sent[i], axis, pairs))
        held = [(kept[i].astype(F32) + got[i].astype(F32)).astype(LOW) for i in range(4)]
        if step < 3:
            held = together(held)
    return [q.reshape(rows, q.shape[-1]) for q in held]


def gather_group(halves):
    held = [h[None, None] for h in halves]
    for step in range(2):
        fresh = [lax.ppermute(held[i], "group", (NEAR, FAR)[(step + i) % 2]) for i in range(2)]
        held = [jnp.concatenate([held[i], fresh[i]], axis=(step + i) % 2) for i in range(2)]
    return [h.reshape(8, *h.shape[3:]) for h in held]


def scatter_group(halves):
    held = [h.reshape(2, 2, 2, *h.shape[1:]) for h in halves]
    for step in range(2):
        fresh = []
        for i in range(2):
            axis = (step + i) % 2
            sent = lax.slice_in_dim(held[i], 1, 2, axis=axis)
            kept = lax.slice_in_dim(held[i], 0, 1, axis=axis)
            got = lax.ppermute(sent, "group", (NEAR, FAR)[axis])
            total = kept.astype(F32) + got.astype(F32)
            fresh.append(total.astype(LOW) if step == 0 else total)
        held = fresh
    return [h.reshape(h.shape[2:]) for h in held]


def sum_everywhere(x):
    steps = [("dp_2", ((0, 1), (1, 0))), *LINKS, ("group", NEAR), ("group", FAR)]
    for axis, pairs in steps:
        x = x + lax.ppermute(x, axis, pairs)
    return x


def dot(left, right, dims=((1,), (0,))):
    return lax.dot_general(left, right, (dims, ((), ())), preferred_element_type=F32)


ROWS = ((0,), (0,))
LAST = ((1,), (1,))
PLAIN = ((1,), (0,))


def split_two(x):
    high = lax.reduce_precision(x, exponent_bits=8, mantissa_bits=7)
    return high.astype(LOW), (x - high).astype(LOW)


def in_two(left, right):
    rows = left.shape[0]
    both_parts = dot(jnp.concatenate(split_two(left), axis=0), right)
    return both_parts[:rows] + both_parts[rows:]


def half_turn(u):
    return jnp.concatenate([u[:, HD // 2 :], u[:, : HD // 2]], axis=1)


def head_forward(raw, gain, cosine, sine):
    scale = lax.rsqrt(jnp.mean(raw * raw, axis=-1, keepdims=True) + norm_eps)
    normed = raw * scale
    gained = normed * gain
    turned = gained * cosine + half_turn(gained) * sine
    return normed, scale, turned.astype(LOW)


def softmax_parts(query, key):
    scores = dot(query, key, LAST) * score_scale
    rows = lax.broadcasted_iota(jnp.int32, scores.shape, 0)
    columns = lax.broadcasted_iota(jnp.int32, scores.shape, 1)
    scores = jnp.where(rows >= columns, scores, masked_score)
    terms = jnp.exp(scores - jnp.max(scores, axis=-1, keepdims=True))
    return terms / jnp.sum(terms, axis=-1, keepdims=True)


def attend_kernel(raw_ref, cos_ref, sin_ref, gain_ref, out_ref):
    cosine, sine = cos_ref[...], sin_ref[...]
    _, _, key = head_forward(raw_ref[:, 2 * HD : 3 * HD], gain_ref[1:2, :], cosine, sine)
    value = raw_ref[:, 3 * HD :].astype(LOW)
    for h in range(2):
        at = slice(h * HD, (h + 1) * HD)
        _, _, query = head_forward(raw_ref[:, at], gain_ref[0:1, :], cosine, sine)
        probs = softmax_parts(query, key).astype(LOW)
        out_ref[:, at] = dot(probs, value).astype(LOW)


def head_backward(grad, normed, scale, gain, cosine, sine):
    back = grad * cosine - half_turn(grad) * sine
    term = jnp.sum(back * normed, axis=0, keepdims=True)
    g = back * gain
    raw = scale * (g - normed * jnp.mean(g * normed, axis=-1, keepdims=True))
    return raw.astype(LOW), term


def attend_back_kernel(raw_ref, grad_ref, cos_ref, sin_ref, gain_ref, out_ref, term_ref):
    cosine, sine = cos_ref[...], sin_ref[...]
    key_hat, key_scale, key = head_forward(
        raw_ref[:, 2 * HD : 3 * HD], gain_ref[1:2, :], cosine, sine
    )
    value = raw_ref[:, 3 * HD :].astype(LOW)
    grad_value = jnp.zeros((SEQ, HD), F32)
    grad_key = jnp.zeros((SEQ, HD), F32)
    query_term = jnp.zeros((1, HD), F32)
    for h in range(2):
        at = slice(h * HD, (h + 1) * HD)
        query_hat, query_scale, query = head_forward(
            raw_ref[:, at], gain_ref[0:1, :], cosine, sine
        )
        probs = softmax_parts(query, key)
        grad_attn = grad_ref[:, at]
        grad_value = grad_value + dot(probs.astype(LOW), grad_attn, ROWS)
        grad_probs = dot(grad_attn, value, LAST)
        inner = jnp.sum(probs * grad_probs, axis=-1, keepdims=True)
        grad_scores = (probs * (grad_probs - inner)).astype(LOW)
        grad_query = dot(grad_scores, key) * score_scale
        grad_key = grad_key + dot(grad_scores, query, ROWS) * score_scale
        raw, term = head_backward(
            grad_query, query_hat, query_scale, gain_ref[0:1, :], cosine, sine
        )
        out_ref[:, at] = raw
        query_term = query_term + term
    raw, key_term = head_backward(grad_key, key_hat, key_scale, gain_ref[1:2, :], cosine, sine)
    out_ref[:, 2 * HD : 3 * HD] = raw
    out_ref[:, 3 * HD :] = grad_value.astype(LOW)
    spare = jnp.zeros((6, HD), F32)
    term_ref[...] = jnp.concatenate([query_term, key_term, spare], axis=0)


def by_sequence(width):
    return pl.BlockSpec((SEQ, width), lambda s: (s, 0))


def whole(rows, width):
    return pl.BlockSpec((rows, width), lambda s: (0, 0))


def attend(raw, cosine, sine, gain_rows):
    tokens = raw.shape[0]
    return pl.pallas_call(
        attend_kernel,
        grid=(tokens // SEQ,),
        in_specs=[by_sequence(4 * HD), by_sequence(HD), by_sequence(HD), whole(8, HD)],
        out_specs=by_sequence(2 * HD),
        out_shape=jax.ShapeDtypeStruct((tokens, 2 * HD), LOW),
        cost_estimate=pl.CostEstimate(
            flops=tokens * SEQ * HD * 8, bytes_accessed=tokens * HD * 32, transcendentals=tokens * 256
        ),
    )(raw, cosine, sine, gain_rows)


def attend_back(raw, grad_attn, cosine, sine, gain_rows):
    tokens = raw.shape[0]
    grad_raw, terms = pl.pallas_call(
        attend_back_kernel,
        grid=(tokens // SEQ,),
        in_specs=[
            by_sequence(4 * HD),
            by_sequence(2 * HD),
            by_sequence(HD),
            by_sequence(HD),
            whole(8, HD),
        ],
        out_specs=[by_sequence(4 * HD), pl.BlockSpec((8, HD), lambda s: (s, 0))],
        out_shape=[
            jax.ShapeDtypeStruct((tokens, 4 * HD), LOW),
            jax.ShapeDtypeStruct((tokens // SEQ * 8, HD), F32),
        ],
        cost_estimate=pl.CostEstimate(
            flops=tokens * SEQ * HD * 24, bytes_accessed=tokens * HD * 40, transcendentals=tokens * 256
        ),
    )(raw, grad_attn, cosine, sine, gain_rows)
    return grad_raw, jnp.sum(terms.reshape(-1, 8, HD), axis=0)


def shared_sum(partial):
    own = partial.shape[0] // 2
    return partial[:own] + swap(partial[own:].astype(LOW)).astype(F32)


def both(x):
    return jnp.concatenate([x, swap(x)], axis=0)


def norm_back(grad_hat, normed, scale):
    return scale * (grad_hat - normed * jnp.mean(grad_hat * normed, axis=-1, keepdims=True))


def cut(x, core, i, width):
    start = (core * 4 + i) * width
    return x[:, start : start + width]


def shards(
    hidden_in,
    out_grad,
    seq_owner,
    token_place,
    matrix_slot,
    weight_slots,
    momentum_slots,
    gains,
    gain_momentum,
):
    slot_count, length = hidden_in.shape[:2]
    tok_count = slot_count * length
    z, y = lax.axis_index("dp_0"), lax.axis_index("dp_1")
    core, group = lax.axis_index("dp_2"), lax.axis_index("group")
    first_core = core == 0
    replica = ((z * 4 + y) * 2 + core) * 4 + group

    def core_pick(zero, one):
        return jnp.where(first_core, zero, one)

    weight_low = weight_slots.astype(LOW)
    slots_top, slots_low = gather_group([weight_low[:, :16], weight_low[:, 16:]])
    projections = []
    for m in range(7):
        slot = matrix_slot[m]
        at = place_of(jnp.bitwise_xor(group, slot // 2)) * 2 + slot % 2
        rows = [
            lax.dynamic_index_in_dim(part, at, 0, keepdims=False)[:, : WIDTHS[m]]
            for part in (slots_top, slots_low)
        ]
        projections.append(jnp.concatenate(rows, axis=0))
    heads_by_core, inner_by_core = [], []
    for c in range(2):
        heads, inner = [], []
        for i in range(4):
            heads += [
                cut(projections[0], c, i, 2 * HD),
                cut(projections[1], c, i, HD),
                cut(projections[2], c, i, HD),
                cut(projections[3], c, i, 2 * HD),
            ]
            inner += [cut(projections[m], c, i, FF // 8) for m in (4, 5, 6)]
        heads_by_core.append(jnp.concatenate(heads, axis=1))
        inner_by_core.append(jnp.concatenate(inner, axis=1))

    def chip_rows(by_core):
        mine = core_pick(by_core[0], by_core[1])
        got = swap(core_pick(by_core[1], by_core[0]))
        return core_pick(
            jnp.concatenate([mine, got], axis=0), jnp.concatenate([got, mine], axis=0)
        )

    heads_rows = chip_rows(heads_by_core)
    inner_rows = chip_rows(inner_by_core)
    HW, IW = 6 * HD, 3 * FF // 8
    w_heads = gather_quarters([heads_rows[:, i * HW : (i + 1) * HW] for i in range(4)])
    w_inner = gather_quarters([inner_rows[:, i * IW : (i + 1) * IW] for i in range(4)])
    w_raw = [w[:, : 4 * HD] for w in w_heads]
    w_out = [w[:, 4 * HD :] for w in w_heads]
    w_gate_up = [w[:, : FF // 4] for w in w_inner]
    w_down = [w[:, FF // 4 :] for w in w_inner]

    column = lax.broadcasted_iota(jnp.int32, (D, D), 1)
    source = lax.broadcasted_iota(jnp.int32, (D, D), 0)
    block = column // 64
    near_z, near_y = block // 8, (block // 4) % 2
    far_z, far_y = (block // 2) % 2, block % 2
    from_z = jnp.bitwise_xor(z, jnp.bitwise_xor(near_z, far_z * 3))
    from_y = jnp.bitwise_xor(y, jnp.bitwise_xor(near_y, far_y * 3))
    reorder = (source == (from_z * 4 + from_y) * 64 + column % 64).astype(LOW)

    live_count = jnp.sum((seq_owner == replica).astype(jnp.int32))
    live_slot = (jnp.arange(slot_count, dtype=jnp.int32) < live_count).astype(F32)
    live_token = jnp.repeat(live_slot, length)[:, None]
    tokens = dot(hidden_in.reshape(tok_count, D), reorder)
    grad_out = dot(out_grad.reshape(tok_count, D), reorder) * live_token
    grad_low = both(grad_out.astype(LOW))
    layer_gains = jnp.dot(
        gains[: 2 * D].reshape(2, D), reorder.astype(F32), precision=lax.Precision.HIGHEST
    )
    gain_one, gain_two = layer_gains[0:1], layer_gains[1:2]
    gain_rows = jnp.pad(gains[2 * D :].reshape(2, HD), ((0, 6), (0, 0)))
    places = both(token_place).astype(F32).reshape(-1, 1)
    exponent = jnp.arange(HD // 2, dtype=F32) * (-2.0 / HD)
    angles = places * jnp.power(rope_base, exponent)[None, :]
    cosine, sine = jnp.cos(angles), jnp.sin(angles)
    cosine = jnp.concatenate([cosine, cosine], axis=1)
    sine = jnp.concatenate([-sine, sine], axis=1)

    scale_one = lax.rsqrt(jnp.mean(tokens * tokens, axis=-1, keepdims=True) + norm_eps)
    normed_one = tokens * scale_one
    input_one = both((normed_one * gain_one).astype(LOW))
    raw = [dot(input_one, w) for w in w_raw]
    attn = [attend(r, cosine, sine, gain_rows) for r in raw]
    branch = sum(dot(a, w, LAST) for a, w in zip(attn, w_out))
    residual = tokens + shared_sum(branch)
    scale_two = lax.rsqrt(jnp.mean(residual * residual, axis=-1, keepdims=True) + norm_eps)
    normed_two = residual * scale_two
    input_two = both((normed_two * gain_two).astype(LOW))
    act, grad_inner, grad_two = [], [], 0.0
    outward = 0.0
    for i in range(4):
        gate_up = dot(input_two, w_gate_up[i])
        gate, up = gate_up[:, : FF // 8], gate_up[:, FF // 8 :]
        sigmoid = jax.nn.sigmoid(gate)
        swish = gate * sigmoid
        act.append((swish * up).astype(LOW))
        grad_act = dot(grad_low, w_down[i])
        slope = sigmoid * (1.0 + gate * (1.0 - sigmoid))
        grad_inner.append(
            jnp.concatenate(
                [(grad_act * up * slope).astype(LOW), (grad_act * swish).astype(LOW)], axis=1
            )
        )
        outward = outward + dot(act[i], w_down[i], LAST)
        grad_two = grad_two + dot(grad_inner[i], w_gate_up[i], LAST)
    result = (residual + shared_sum(outward)) * live_token
    hidden_out = dot(result.astype(LOW), reorder, LAST).astype(LOW)

    inner_terms = [
        jnp.concatenate(
            [
                dot(input_two, grad_inner[i], ROWS).astype(LOW),
                dot(grad_low, act[i], ROWS).astype(LOW),
            ],
            axis=1,
        )
        for i in range(4)
    ]
    inner_sums = scatter_quarters(inner_terms)
    grad_two = shared_sum(grad_two)
    gain_two_term = jnp.sum(grad_two * normed_two, axis=0, keepdims=True)
    grad_residual = grad_out + norm_back(grad_two * gain_two, normed_two, scale_two)
    branch_low = both(grad_residual.astype(LOW))
    grad_one, head_terms, grad_raw = 0.0, 0.0, []
    for i in range(4):
        grad_attn = dot(branch_low, w_out[i]).astype(LOW)
        fresh, term = attend_back(raw[i], grad_attn, cosine, sine, gain_rows)
        grad_raw.append(fresh)
        head_terms = head_terms + term
        grad_one = grad_one + dot(fresh, w_raw[i], LAST)
    heads_terms = [
        jnp.concatenate(
            [
                dot(input_one, grad_raw[i], ROWS).astype(LOW),
                dot(branch_low, attn[i], ROWS).astype(LOW),
            ],
            axis=1,
        )
        for i in range(4)
    ]
    heads_sums = scatter_quarters(heads_terms)
    grad_one = shared_sum(grad_one)
    gain_one_term = jnp.sum(grad_one * normed_one, axis=0, keepdims=True)
    in_grad = grad_residual + norm_back(grad_one * gain_one, normed_one, scale_one)
    in_high, in_low = split_two(in_grad)
    in_grad = dot(in_high, reorder, LAST) + dot(in_low, reorder, LAST)
    layer_terms = lax.dot_general(
        jnp.concatenate([gain_one_term, gain_two_term], axis=0),
        reorder.astype(F32),
        (LAST, ((), ())),
        precision=lax.Precision.HIGHEST,
    )
    gain_term = jnp.concatenate([layer_terms.reshape(-1), head_terms[:2].reshape(-1)])

    sums = jnp.concatenate([*heads_sums, *inner_sums], axis=1)
    kept = core_pick(sums[:32], sums[32:])
    got = swap(core_pick(sums[32:], sums[:32]))
    by_core = (core_pick(kept, got), core_pick(got, kept))
    heads_at = ((0, 2 * HD), (2 * HD, HD), (3 * HD, HD), (4 * HD, 2 * HD))
    projections = []
    for m in range(7):
        pieces = []
        for c in range(2):
            for i in range(4):
                if m < 4:
                    start, width = heads_at[m]
                    start = start + i * HW
                else:
                    width = FF // 8
                    start = 4 * HW + i * IW + (m - 4) * width
                pieces.append(by_core[c][:, start : start + width])
        pieces.append(jnp.zeros((32, FF - WIDTHS[m]), LOW))
        projections.append(jnp.concatenate(pieces, axis=1))
    routed = []
    for mask in MASKS:
        for j in range(2):
            slot = jnp.bitwise_xor(group, mask) * 2 + j
            held = jnp.zeros((32, FF), LOW)
            for m in range(7):
                held = jnp.where(matrix_slot[m] == slot, projections[m], held)
            routed.append(held)
    routed = jnp.stack(routed)
    weight_grad = jnp.concatenate(scatter_group([routed[:, :16], routed[:, 16:]]), axis=1)

    own_ids = group * 2 + jnp.arange(2, dtype=jnp.int32)
    own_width = jnp.zeros((2,), jnp.int32)
    for m in range(7):
        own_width = own_width + jnp.where(own_ids == matrix_slot[m], WIDTHS[m], 0).astype(jnp.int32)
    column_mask = (jnp.arange(FF, dtype=jnp.int32)[None, :] < own_width[:, None]).astype(F32)
    column_mask = column_mask[:, None, :]
    momentum_new = column_mask * (momentum_keep * momentum_slots + weight_grad)
    direction = (weight_grad + momentum_keep * momentum_new).astype(LOW)

    mine = core_pick(direction[0], direction[1])
    got = swap(core_pick(direction[1], direction[0]))
    rows = core_pick(jnp.concatenate([mine, got], axis=0), jnp.concatenate([got, mine], axis=0))
    QW = FF // 4
    matrix = gather_quarters([rows[:, i * QW : (i + 1) * QW] for i in range(4)])
    *matrix, gain_term = together([*matrix, gain_term])
    gram = sum(dot(x, x, LAST) for x in matrix)
    eye = (column == source).astype(F32)
    inverse = 1.0 / (jnp.sqrt(jnp.sum(gram * eye)) + frob_eps)
    gram = gram * (inverse * inverse)
    own_rows = eye[:64]
    for sweep in range(NS_ITERS):
        gram_high, gram_low = split_two(gram)
        if sweep == NS_ITERS - 1:
            once = in_two(own_rows, gram_high)
            twice = in_two(once, gram_high)
            own_rows = coef_linear * own_rows + coef_square * once + coef_quartic * twice
            break
        square = dot(gram_high, gram_high)
        poly = (coef_square * gram_high.astype(F32) + coef_quartic * square).astype(LOW)
        if sweep == 0:
            own_rows = coef_linear * own_rows + poly[:64].astype(F32)
        else:
            own_rows = coef_linear * own_rows + in_two(own_rows, poly)
        mixed = dot(gram_high, poly) + dot(gram_low, poly)
        mixed_high, mixed_low = split_two(mixed)
        gram = (
            (coef_linear * coef_linear) * gram
            + (2.0 * coef_linear) * mixed
            + (dot(mixed_high, poly) + dot(mixed_low, poly))
        )
    own_rows = own_rows * inverse
    iterate = jnp.concatenate([in_two(own_rows, x) for x in matrix], axis=1).astype(LOW)
    kept = core_pick(iterate[:32], iterate[32:])
    got = swap(core_pick(iterate[32:], iterate[:32]))
    iterate = jnp.stack([core_pick(kept, got), core_pick(got, kept)]).astype(F32)
    update_scale = 0.2 * jnp.sqrt(jnp.maximum(own_width, D).astype(F32))
    weight_new = column_mask * (
        weight_slots * (1.0 - learn_rate * weight_decay)
        - learn_rate * update_scale[:, None, None] * iterate
    )

    gain_grad = sum_everywhere(gain_term)
    gain_momentum_new = momentum_keep * gain_momentum + gain_grad
    gain_step = gain_grad + momentum_keep * gain_momentum_new
    bounds = (0, D, 2 * D, 2 * D + HD, 2 * D + 2 * HD)
    scaled_parts = []
    for number in range(4):
        segment = gain_step[bounds[number] : bounds[number + 1]]
        scaled_parts.append(segment * lax.rsqrt(jnp.mean(segment * segment) + norm_eps))
    gain_new = gains - gain_rate * jnp.concatenate(scaled_parts)
    shape = (slot_count, length, D)
    return (
        hidden_out.reshape(shape),
        in_grad.reshape(shape),
        weight_grad,
        momentum_new,
        weight_new,
        gain_grad,
        gain_momentum_new,
        gain_new,
    )


def solution(mesh):
    finer = Mesh(
        mesh.devices.reshape(4, 4, 2, mesh.shape["group"]), ("dp_0", "dp_1", "dp_2", "group")
    )
    in_specs = (
        P(DP_GROUP, None, None),
        P(DP_GROUP, None, None),
        P(),
        P(DP_GROUP, None),
        P(),
        P("group", ("dp_0", "dp_1", "dp_2"), None),
        P("group", ("dp_0", "dp_1", "dp_2"), None),
        P(),
        P(),
    )
    out_specs = (
        P(DP_GROUP, None, None),
        P(DP_GROUP, None, None),
        P("group", ("dp_0", "dp_1", "dp_2"), None),
        P("group", ("dp_0", "dp_1", "dp_2"), None),
        P("group", ("dp_0", "dp_1", "dp_2"), None),
        P(),
        P(),
        P(),
    )
    return jax.shard_map(
        shards, mesh=finer, in_specs=in_specs, out_specs=out_specs, check_vma=False
    )
```

time: 1400 us -> 785 us (0.56)
  waiting for transfers between devices: 912 us -> 203 us
  starting transfers between devices: 1.25 us -> 139 us
  blocking collectives: 80.3 us -> 0 us
  local copies, waits for them, and re-layouts: 142 us -> 65.8 us
  Pallas kernels: 0 us -> 52 us
  other arithmetic: 37.8 us -> 75 us
  between operations: 31.2 us -> 61.5 us
    all_gather x13 -> x0, waiting for transfers between devices: 736 us -> none  [the longest x5 308 us: shards(): full_rows = lax.all_gather(iterate, DP, axis=1, tiled=True)]
    ppermute x0 -> x109, waiting for transfers between devices: none -> 203 us  [the longest x48 88.5 us: gather_steps(): fresh.append(lax.ppermute(quarters[i], axis, pairs))]
    reduce_scatter x2 -> x0, waiting for transfers between devices: 176 us -> none  [the longest x1 156 us: shards(): lax.psum_scatter(jnp.concatenate(blocks_out, axis=1).astype(jnp.bfloat16)...]
    ppermute x0 -> x109, starting transfers between devices: none -> 139 us  [the longest x48 46.7 us: gather_steps(): fresh.append(lax.ppermute(quarters[i], axis, pairs))]
    transpose x2 -> x0, local copies, waits for them, and re-layouts: 67.1 us -> none  [the longest x1 33.6 us: gather_in_order(): pieces = pieces.transpose(*back, *range(len(axes), pieces.ndim))]
    psum x1 -> x0, blocking collectives: 64.9 us -> none  [shards(): gain_grad = lax.psum(gain_term, DP_GROUP)]
    pallas_call x0 -> x8, Pallas kernels: none -> 52 us  [the longest x4 29.4 us: attend_back(): pl.pallas_call(attend_back_kernel, grid=(tokens // SEQ,), in_specs=[by_se...]
    concatenate x0 -> x68, other arithmetic: none -> 32.2 us  [the longest x48 18.3 us: gather_steps(): jnp.concatenate([quarters[i], fresh[i]], axis=(step + i) % 4)]
  transfers between devices with their start and end apart: 15 -> 109, of which waited for: 14 -> 57; matrix products, arithmetic and copies ran while one was open for 3% -> 27% of each run, Pallas kernels for 0% -> 7%
where the time goes in v1:
time: 785 us; the launch traced here: 770 us
  waiting for transfers between devices  203 us (26%)
  matrix products  174 us (22%)
  starting transfers between devices  139 us (18%)
  other arithmetic  75 us (10%)
  local copies, waits for them, and re-layouts  65.8 us (8%)
  between operations  61.5 us (8%)
  Pallas kernels  52 us (7%)
    dot_general x86, matrix products, dot(): lax.dot_general(left, right, (dims, ((), ())), preferred_element_type=F32)  170 us
    ppermute x48, waiting for transfers between devices, gather_steps(): fresh.append(lax.ppermute(quarters[i], axis, pairs))  88.5 us
    ppermute x32, waiting for transfers between devices, scatter_quarters(): got.append(lax.ppermute(sent[i], axis, pairs))  74.4 us
    ppermute x48, starting transfers between devices, gather_steps(): fresh.append(lax.ppermute(quarters[i], axis, pairs))  46.7 us
    ppermute x14, starting transfers between devices, swap(): return lax.ppermute(x, 'dp_2', ((0, 1), (1, 0)))  44.9 us
    pallas_call x4, Pallas kernels, attend_back(): pl.pallas_call(attend_back_kernel, grid=(tokens // SEQ,), in_specs=[by_se...  29.4 us
    ppermute x32, starting transfers between devices, scatter_quarters(): got.append(lax.ppermute(sent[i], axis, pairs))  26.7 us
    pallas_call x4, Pallas kernels, attend(): pl.pallas_call(attend_kernel, grid=(tokens // SEQ,), in_specs=[by_sequenc...  22.6 us
  transfers between devices with their start and end apart: 109, of which 57 were waited for; matrix products, arithmetic and copies ran while one was open for 27% of the time, Pallas kernels for 7%

profile of v1, /device:TPU:1, one launch (start us, length us, event | category | flops | bytes accessed | tf_op | source)
XLA Modules:
  0.0 770.3 jit_solution(15858818043883766189)
XLA Ops:
  33.6 5.0 sqrt_multiply_fusion
  44.3 7.6 collective-permute-done.4
  71.5 5.3 collective-permute-done.27
  77.4 4.6 collective-permute-done.28
  82.4 4.9 collective-permute-done.29
  107.9 8.9 %collective-permute-start.43 = (bf16[256,1024]{1,0:T(8,128)(2,1)}, bf16[256,1024]{1,0:T(8,128)(2,1)}, u32[]{:S(2)}, u32[]{:S(2)}) collective-permute-start(bf16[256,1024]{1,0:T(8,128)(2,1)} %get-tuple-element.344), channel_id=1, source_target_pairs={{0,4},{4,0},{1,5},{5,1},{2,6},{6,2},{3,7},{7,3},{8,12},{12,8},{9,1... | collective-permute-start | bytes 1572872 | tf_op jit(solution)/shard_map/ppermute | solution.py:47
  122.6 5.2 collective-permute-done.36
  133.3 13.7 %collective-permute-done.21 = bf16[2,1,2,2,64,768]{5,4,3,2,1,0:T(8,128)(2,1)S(1)} collective-permute-done((bf16[2,1,2,2,64,768]{5,4,3,2,1,0:T(8,128)(2,1)S(1)}, bf16[2,1,2,2,64,768]{5,4,3,2,1,0:T(8,128)(2,1)S(1)}, u32[]{:S(2)}, u32[]{:S(2)}) %collective-permute-start.21) | collective-permute-done | bytes 786464 | tf_op jit(solution)/shard_map/ppermute | solution.py:58
  152.8 5.7 shard_map.154
  164.1 5.6 shard_map.152
  175.4 5.6 shard_map.153
  193.6 5.7 shard_map.155
  204.1 4.8 collective-permute-start.23
  256.1 20.4 %collective-permute-done.39 = bf16[1,2,2,2,64,1152]{5,4,3,2,1,0:T(8,128)(2,1)S(1)} collective-permute-done((bf16[1,2,2,2,64,1152]{5,4,3,2,1,0:T(8,128)(2,1)}, bf16[1,2,2,2,64,1152]{5,4,3,2,1,0:T(8,128)(2,1)S(1)}, u32[]{:S(2)}, u32[]{:S(2)}) %collective-permute-start.39) | collective-permute-done | bytes 1179680 | tf_op jit(solution)/shard_map/ppermute | solution.py:58
  328.7 4.4 copy.50
  359.7 7.4 shard_map.158
  372.6 7.3 shard_map.156
  385.6 7.3 shard_map.157
  398.5 7.3 shard_map.159
  464.4 11.3 %collective-permute-done.67 = bf16[1,1,2,2,64,1152]{5,4,3,2,1,0:T(8,128)(2,1)} collective-permute-done((bf16[1,1,2,2,64,1152]{5,4,3,2,1,0:T(8,128)(2,1)}, bf16[1,1,2,2,64,1152]{5,4,3,2,1,0:T(8,128)(2,1)}, u32[]{:S(2)}, u32[]{:S(2)}) %collective-permute-start.67) | collective-permute-done | bytes 589856 | tf_op jit(solution)/shard_map/ppermute | solution.py:83
  479.2 11.1 %collective-permute-done.69 = bf16[2,2,1,1,64,1152]{5,4,3,2,1,0:T(8,128)(2,1)S(1)} collective-permute-done((bf16[2,2,1,1,64,1152]{5,4,3,2,1,0:T(8,128)(2,1)S(1)}, bf16[2,2,1,1,64,1152]{5,4,3,2,1,0:T(8,128)(2,1)S(1)}, u32[]{:S(2)}, u32[]{:S(2)}) %collective-permute-start.69) | collective-permute-done | bytes 589856 | tf_op jit(solution)/shard_map/ppermute | solution.py:83
  496.3 11.9 %collective-permute-done.49 = bf16[2,2,1,2,64,768]{5,4,3,2,1,0:T(8,128)(2,1)S(1)} collective-permute-done((bf16[2,2,1,2,64,768]{5,4,3,2,1,0:T(8,128)(2,1)S(1)}, bf16[2,2,1,2,64,768]{5,4,3,2,1,0:T(8,128)(2,1)S(1)}, u32[]{:S(2)}, u32[]{:S(2)}) %collective-permute-start.49) | collective-permute-done | bytes 786464 | tf_op jit(solution)/shard_map/ppermute | solution.py:83
  517.4 5.6 collective-permute-done.51
  524.4 6.5 collective-permute-done.53
  546.9 4.9 collective-permute-done.60
  565.6 15.0 %collective-permute-start.79 = (bf16[32,7680]{1,0:T(8,128)(2,1)S(1)}, bf16[32,7680]{1,0:T(8,128)(2,1)S(1)}, u32[]{:S(2)}, u32[]{:S(2)}) collective-permute-start(bf16[32,7680]{1,0:T(8,128)(2,1)S(1)} %broadcast_select_fusion.2), channel_id=1, source_target_pairs={{0,4},{4,0},{1,5},{5,1},{2,6},{6,2},{3,7},{7,3},{8,12},{12,8},{9,1... | collective-permute-start | bytes 1474568 | tf_op jit(solution)/shard_map/ppermute | solution.py:47
  590.7 11.2 %collective-permute-done.82 = bf16[2,1,2,16,3072]{4,3,2,1,0:T(8,128)(2,1)S(1)} collective-permute-done((bf16[2,1,2,16,3072]{4,3,2,1,0:T(8,128)(2,1)S(1)}, bf16[2,1,2,16,3072]{4,3,2,1,0:T(8,128)(2,1)S(1)}, u32[]{:S(2)}, u32[]{:S(2)}) %collective-permute-start.82) | collective-permute-done | bytes 393248 | tf_op jit(solution)/shard_map/ppermute | solution.py:106
  649.8 7.8 %collective-permute-done.97 = bf16[2,2,2,1,64,768]{5,4,3,2,1,0:T(8,128)(2,1)S(1)} collective-permute-done((bf16[2,2,2,1,64,768]{5,4,3,2,1,0:T(8,128)(2,1)S(1)}, bf16[2,2,2,1,64,768]{5,4,3,2,1,0:T(8,128)(2,1)S(1)}, u32[]{:S(2)}, u32[]{:S(2)}) %collective-permute-start.97) | collective-permute-done | bytes 786464 | tf_op jit(solution)/shard_map/ppermute | solution.py:58
  664.1 4.6 select_reduce_fusion
  669.5 7.3 add_convert_fusion.3
  730.7 8.3 %collective-permute-start.102 = (f32[2304]{0:T(1024)S(1)}, f32[2304]{0:T(1024)S(1)}, u32[]{:S(2)}, u32[]{:S(2)}) collective-permute-start(f32[2304]{0:T(1024)S(1)} %pad_maximum_fusion.92), channel_id=1, source_target_pairs={{0,4},{4,0},{1,5},{5,1},{2,6},{6,2},{3,7},{7,3},{8,12},{12,8},{9,1... | collective-permute-start | bytes 27656 | tf_op jit(solution)/shard_map/ppermute | solution.py:116
  756.1 6.5 collective-permute-start.101
  (792 shorter events, 460.0 us)
Async XLA Ops:
  1.9 39.5 %collective-permute-start.3 = (bf16[1,1,2,16,3072]{4,3,2,1,0:T(8,128)(2,1)S(1)}, bf16[1,1,2,16,3072]{4,3,2,1,0:T(8,128)(2,1)S(1)}, u32[]{:S(2)}, u32[]{:S(2)}) collective-permute-start(bf16[1,1,2,16,3072]{4,3,2,1,0:T(8,128)(2,1)S(1)} %get-tuple-element.311), channel_id=1, source_target_pairs={{0,3},{3,0},{1,2},{2,1},{4,7},{7,4},{5,6},{6,5},{8,11},{11,8},{9,1... | collective-permute-start | bytes 589832 | tf_op jit(solution)/shard_map/ppermute | solution.py:93
  5.3 37.8 %collective-permute-start.1 = (bf16[1,1,2,16,3072]{4,3,2,1,0:T(8,128)(2,1)S(1)}, bf16[1,1,2,16,3072]{4,3,2,1,0:T(8,128)(2,1)S(1)}, u32[]{:S(2)}, u32[]{:S(2)}) collective-permute-start(bf16[1,1,2,16,3072]{4,3,2,1,0:T(8,128)(2,1)S(1)} %get-tuple-element.310), channel_id=1, source_target_pairs={{0,1},{1,0},{2,3},{3,2},{4,5},{5,4},{6,7},{7,6},{8,9},{9,8},{10,11... | collective-permute-start | bytes 589832 | tf_op jit(solution)/shard_map/ppermute | solution.py:93
  11.6 136.0 %collective-permute-start = (bf16[256,1024]{1,0:T(8,128)(2,1)}, bf16[256,1024]{1,0:T(8,128)(2,1)}, u32[]{:S(2)}, u32[]{:S(2)}) collective-permute-start(bf16[256,1024]{1,0:T(8,128)(2,1)} %multiply_convert_fusion.1), channel_id=1, source_target_pairs={{0,4},{4,0},{1,5},{5,1},{2,6},{6,2},{3,7},{7,3},{8,12},{12,8},{9,1... | collective-permute-start | bytes 1572872 | tf_op jit(solution)/shard_map/ppermute | solution.py:47
  12.8 28.7 %collective-permute-start.19 = (s32[2,128]{1,0:T(2,128)S(1)}, s32[2,128]{1,0:T(2,128)S(1)}, u32[]{:S(2)}, u32[]{:S(2)}) collective-permute-start(s32[2,128]{1,0:T(2,128)S(1)} %copy-done.82), channel_id=1, source_target_pairs={{0,4},{4,0},{1,5},{5,1},{2,6},{6,2},{3,7},{7,3},{8,12},{12,8},{9,1... | collective-permute-start | bytes 3080 | tf_op jit(solution)/shard_map/ppermute | solution.py:47
  67.9 19.3 %collective-permute-start.10 = (bf16[2,1,1,1,64,768]{5,4,3,2,1,0:T(8,128)(2,1)S(1)}, bf16[2,1,1,1,64,768]{5,4,3,2,1,0:T(8,128)(2,1)S(1)}, u32[]{:S(2)}, u32[]{:S(2)}) collective-permute-start(bf16[2,1,1,1,64,768]{5,4,3,2,1,0:T(8,128)(2,1)S(1)} %pad_maximum_fusion.79), channel_id=1, source_target_pairs={{0,8},{8,0},{16,24},{24,16},{1,9},{9,1},{17,25},{25,17},{2,10},{10... | collective-permute-start | bytes 589832 | tf_op jit(solution)/shard_map/ppermute | solution.py:58
  68.0 19.4 %collective-permute-start.11 = (bf16[1,2,1,1,64,768]{5,4,3,2,1,0:T(8,128)(2,1)S(1)}, bf16[1,2,1,1,64,768]{5,4,3,2,1,0:T(8,128)(2,1)S(1)}, u32[]{:S(2)}, u32[]{:S(2)}) collective-permute-start(bf16[1,2,1,1,64,768]{5,4,3,2,1,0:T(8,128)(2,1)S(1)} %pad_maximum_fusion.80), channel_id=1, source_target_pairs={{0,96},{96,0},{32,64},{64,32},{1,97},{97,1},{33,65},{65,33},{2,98}... | collective-permute-start | bytes 589832 | tf_op jit(solution)/shard_map/ppermute | solution.py:58
  68.8 19.3 %collective-permute-start.12 = (bf16[1,1,2,1,64,768]{5,4,3,2,1,0:T(8,128)(2,1)S(1)}, bf16[1,1,2,1,64,768]{5,4,3,2,1,0:T(8,128)(2,1)S(1)}, u32[]{:S(2)}, u32[]{:S(2)}) collective-permute-start(bf16[1,1,2,1,64,768]{5,4,3,2,1,0:T(8,128)(2,1)S(1)} %pad_maximum_fusion.81), channel_id=1, source_target_pairs={{0,24},{24,0},{8,16},{16,8},{1,25},{25,1},{9,17},{17,9},{2,26},{26... | collective-permute-start | bytes 589832 | tf_op jit(solution)/shard_map/ppermute | solution.py:58
  99.8 19.0 %collective-permute-start.34 = (bf16[2,2,1,1,64,1152]{5,4,3,2,1,0:T(8,128)(2,1)S(1)}, bf16[2,2,1,1,64,1152]{5,4,3,2,1,0:T(8,128)(2,1)S(1)}, u32[]{:S(2)}, u32[]{:S(2)}) collective-permute-start(bf16[2,2,1,1,64,1152]{5,4,3,2,1,0:T(8,128)(2,1)S(1)} %pad_maximum_fusion.43), channel_id=1, source_target_pairs={{0,96},{96,0},{32,64},{64,32},{1,97},{97,1},{33,65},{65,33},{2,98}... | collective-permute-start | bytes 1769480 | tf_op jit(solution)/shard_map/ppermute | solution.py:58
  107.9 171.2 %collective-permute-start.43 = (bf16[256,1024]{1,0:T(8,128)(2,1)}, bf16[256,1024]{1,0:T(8,128)(2,1)}, u32[]{:S(2)}, u32[]{:S(2)}) collective-permute-start(bf16[256,1024]{1,0:T(8,128)(2,1)} %get-tuple-element.344), channel_id=1, source_target_pairs={{0,4},{4,0},{1,5},{5,1},{2,6},{6,2},{3,7},{7,3},{8,12},{12,8},{9,1... | collective-permute-start | bytes 1572872 | tf_op jit(solution)/shard_map/ppermute | solution.py:47
  121.4 25.5 %collective-permute-start.21 = (bf16[2,1,2,2,64,768]{5,4,3,2,1,0:T(8,128)(2,1)S(1)}, bf16[2,1,2,2,64,768]{5,4,3,2,1,0:T(8,128)(2,1)S(1)}, u32[]{:S(2)}, u32[]{:S(2)}) collective-permute-start(bf16[2,1,2,2,64,768]{5,4,3,2,1,0:T(8,128)(2,1)S(1)} %pad_maximum_fusion.32), channel_id=1, source_target_pairs={{0,8},{8,0},{16,24},{24,16},{1,9},{9,1},{17,25},{25,17},{2,10},{10... | collective-permute-start | bytes 2359304 | tf_op jit(solution)/shard_map/ppermute | solution.py:58
  127.8 30.6 %collective-permute-start.18 = (bf16[2,2,2,1,64,768]{5,4,3,2,1,0:T(8,128)(2,1)}, bf16[2,2,2,1,64,768]{5,4,3,2,1,0:T(8,128)(2,1)}, u32[]{:S(2)}, u32[]{:S(2)}) collective-permute-start(bf16[2,2,2,1,64,768]{5,4,3,2,1,0:T(8,128)(2,1)} %pad_maximum_fusion.30), channel_id=1, source_target_pairs={{0,24},{24,0},{8,16},{16,8},{1,25},{25,1},{9,17},{17,9},{2,26},{26... | collective-permute-start | bytes 2359304 | tf_op jit(solution)/shard_map/ppermute | solution.py:58
  131.5 38.2 %collective-permute-start.20 = (bf16[1,2,2,2,64,768]{5,4,3,2,1,0:T(8,128)(2,1)}, bf16[1,2,2,2,64,768]{5,4,3,2,1,0:T(8,128)(2,1)}, u32[]{:S(2)}, u32[]{:S(2)}) collective-permute-start(bf16[1,2,2,2,64,768]{5,4,3,2,1,0:T(8,128)(2,1)} %pad_maximum_fusion.31), channel_id=1, source_target_pairs={{0,32},{32,0},{64,96},{96,64},{1,33},{33,1},{65,97},{97,65},{2,34}... | collective-permute-start | bytes 2359304 | tf_op jit(solution)/shard_map/ppermute | solution.py:58
  146.9 41.7 %collective-permute-start.22 = (bf16[2,2,1,2,64,768]{5,4,3,2,1,0:T(8,128)(2,1)}, bf16[2,2,1,2,64,768]{5,4,3,2,1,0:T(8,128)(2,1)}, u32[]{:S(2)}, u32[]{:S(2)}) collective-permute-start(bf16[2,2,1,2,64,768]{5,4,3,2,1,0:T(8,128)(2,1)} %pad_maximum_fusion.33), channel_id=1, source_target_pairs={{0,96},{96,0},{32,64},{64,32},{1,97},{97,1},{33,65},{65,33},{2,98}... | collective-permute-start | bytes 2359304 | tf_op jit(solution)/shard_map/ppermute | solution.py:58
  147.6 103.8 %collective-permute-start.40 = (bf16[2,1,2,2,64,1152]{5,4,3,2,1,0:T(8,128)(2,1)}, bf16[2,1,2,2,64,1152]{5,4,3,2,1,0:T(8,128)(2,1)}, u32[]{:S(2)}, u32[]{:S(2)}) collective-permute-start(bf16[2,1,2,2,64,1152]{5,4,3,2,1,0:T(8,128)(2,1)} %pad_maximum_fusion.21), channel_id=1, source_target_pairs={{0,8},{8,0},{16,24},{24,16},{1,9},{9,1},{17,25},{25,17},{2,10},{10... | collective-permute-start | bytes 3538952 | tf_op jit(solution)/shard_map/ppermute | solution.py:58
  204.1 45.0 %collective-permute-start.23 = (bf16[256,1024]{1,0:T(8,128)(2,1)S(1)}, bf16[256,1024]{1,0:T(8,128)(2,1)S(1)}, u32[]{:S(2)}, u32[]{:S(2)}) collective-permute-start(bf16[256,1024]{1,0:T(8,128)(2,1)S(1)} %slice.2435), channel_id=1, source_target_pairs={{0,4},{4,0},{1,5},{5,1},{2,6},{6,2},{3,7},{7,3},{8,12},{12,8},{9,1... | collective-permute-start | bytes 1572872 | tf_op jit(solution)/shard_map/ppermute | solution.py:47
  209.0 45.2 %collective-permute-start.38 = (bf16[2,2,2,1,64,1152]{5,4,3,2,1,0:T(8,128)(2,1)}, bf16[2,2,2,1,64,1152]{5,4,3,2,1,0:T(8,128)(2,1)}, u32[]{:S(2)}, u32[]{:S(2)}) collective-permute-start(bf16[2,2,2,1,64,1152]{5,4,3,2,1,0:T(8,128)(2,1)} %pad_maximum_fusion.19), channel_id=1, source_target_pairs={{0,24},{24,0},{8,16},{16,8},{1,25},{25,1},{9,17},{17,9},{2,26},{26... | collective-permute-start | bytes 3538952 | tf_op jit(solution)/shard_map/ppermute | solution.py:58
  249.0 27.6 %collective-permute-start.39 = (bf16[1,2,2,2,64,1152]{5,4,3,2,1,0:T(8,128)(2,1)}, bf16[1,2,2,2,64,1152]{5,4,3,2,1,0:T(8,128)(2,1)S(1)}, u32[]{:S(2)}, u32[]{:S(2)}) collective-permute-start(bf16[1,2,2,2,64,1152]{5,4,3,2,1,0:T(8,128)(2,1)} %pad_maximum_fusion.20), channel_id=1, source_target_pairs={{0,32},{32,0},{64,96},{96,64},{1,33},{33,1},{65,97},{97,65},{2,34}... | collective-permute-start | bytes 3538952 | tf_op jit(solution)/shard_map/ppermute | solution.py:58
  249.1 28.8 %collective-permute-start.41 = (bf16[2,2,1,2,64,1152]{5,4,3,2,1,0:T(8,128)(2,1)}, bf16[2,2,1,2,64,1152]{5,4,3,2,1,0:T(8,128)(2,1)S(1)}, u32[]{:S(2)}, u32[]{:S(2)}) collective-permute-start(bf16[2,2,1,2,64,1152]{5,4,3,2,1,0:T(8,128)(2,1)} %pad_maximum_fusion.22), channel_id=1, source_target_pairs={{0,96},{96,0},{32,64},{64,32},{1,97},{97,1},{33,65},{65,33},{2,98}... | collective-permute-start | bytes 3538952 | tf_op jit(solution)/shard_map/ppermute | solution.py:58
  251.4 26.7 %collective-permute-start.24 = (bf16[256,1024]{1,0:T(8,128)(2,1)S(1)}, bf16[256,1024]{1,0:T(8,128)(2,1)S(1)}, u32[]{:S(2)}, u32[]{:S(2)}) collective-permute-start(bf16[256,1024]{1,0:T(8,128)(2,1)S(1)} %multiply_convert_fusion), channel_id=1, source_target_pairs={{0,4},{4,0},{1,5},{5,1},{2,6},{6,2},{3,7},{7,3},{8,12},{12,8},{9,1... | collective-permute-start | bytes 1572872 | tf_op jit(solution)/shard_map/ppermute | solution.py:47
  294.1 58.2 %collective-permute-start.42 = (bf16[256,1024]{1,0:T(8,128)(2,1)S(1)}, bf16[256,1024]{1,0:T(8,128)(2,1)}, u32[]{:S(2)}, u32[]{:S(2)}) collective-permute-start(bf16[256,1024]{1,0:T(8,128)(2,1)S(1)} %slice.2434), channel_id=1, source_target_pairs={{0,4},{4,0},{1,5},{5,1},{2,6},{6,2},{3,7},{7,3},{8,12},{12,8},{9,1... | collective-permute-start | bytes 1572872 | tf_op jit(solution)/shard_map/ppermute | solution.py:47
  300.5 47.3 %collective-permute-start.44 = (bf16[256,1024]{1,0:T(8,128)(2,1)}, bf16[256,1024]{1,0:T(8,128)(2,1)S(1)}, u32[]{:S(2)}, u32[]{:S(2)}) collective-permute-start(bf16[256,1024]{1,0:T(8,128)(2,1)} %slice.2433), channel_id=1, source_target_pairs={{0,4},{4,0},{1,5},{5,1},{2,6},{6,2},{3,7},{7,3},{8,12},{12,8},{9,1... | collective-permute-start | bytes 1572872 | tf_op jit(solution)/shard_map/ppermute | solution.py:47
  311.0 139.4 %collective-permute-start.63 = (bf16[1,2,2,2,64,1152]{5,4,3,2,1,0:T(8,128)(2,1)}, bf16[1,2,2,2,64,1152]{5,4,3,2,1,0:T(8,128)(2,1)}, u32[]{:S(2)}, u32[]{:S(2)}) collective-permute-start(bf16[1,2,2,2,64,1152]{5,4,3,2,1,0:T(8,128)(2,1)} %bitcast.514), channel_id=1, source_target_pairs={{0,32},{32,0},{64,96},{96,64},{1,33},{33,1},{65,97},{97,65},{2,34}... | collective-permute-start | bytes 3538952 | tf_op jit(solution)/shard_map/ppermute | solution.py:83
  324.1 116.6 %collective-permute-start.64 = (bf16[2,1,2,2,64,1152]{5,4,3,2,1,0:T(8,128)(2,1)}, bf16[2,1,2,2,64,1152]{5,4,3,2,1,0:T(8,128)(2,1)}, u32[]{:S(2)}, u32[]{:S(2)}) collective-permute-start(bf16[2,1,2,2,64,1152]{5,4,3,2,1,0:T(8,128)(2,1)} %slice.1390), channel_id=1, source_target_pairs={{0,8},{8,0},{16,24},{24,16},{1,9},{9,1},{17,25},{25,17},{2,10},{10... | collective-permute-start | bytes 3538952 | tf_op jit(solution)/shard_map/ppermute | solution.py:83
  335.6 108.7 %collective-permute-start.65 = (bf16[2,2,1,2,64,1152]{5,4,3,2,1,0:T(8,128)(2,1)}, bf16[2,2,1,2,64,1152]{5,4,3,2,1,0:T(8,128)(2,1)}, u32[]{:S(2)}, u32[]{:S(2)}) collective-permute-start(bf16[2,2,1,2,64,1152]{5,4,3,2,1,0:T(8,128)(2,1)} %slice.1392), channel_id=1, source_target_pairs={{0,96},{96,0},{32,64},{64,32},{1,97},{97,1},{33,65},{65,33},{2,98}... | collective-permute-start | bytes 3538952 | tf_op jit(solution)/shard_map/ppermute | solution.py:83
  347.8 100.1 %collective-permute-start.66 = (bf16[2,2,2,1,64,1152]{5,4,3,2,1,0:T(8,128)(2,1)}, bf16[2,2,2,1,64,1152]{5,4,3,2,1,0:T(8,128)(2,1)}, u32[]{:S(2)}, u32[]{:S(2)}) collective-permute-start(bf16[2,2,2,1,64,1152]{5,4,3,2,1,0:T(8,128)(2,1)} %slice.1394), channel_id=1, source_target_pairs={{0,24},{24,0},{8,16},{16,8},{1,25},{25,1},{9,17},{17,9},{2,26},{26... | collective-permute-start | bytes 3538952 | tf_op jit(solution)/shard_map/ppermute | solution.py:83
  410.8 169.9 %collective-permute-start.46 = (bf16[256,1024]{1,0:T(8,128)(2,1)}, bf16[256,1024]{1,0:T(8,128)(2,1)S(1)}, u32[]{:S(2)}, u32[]{:S(2)}) collective-permute-start(bf16[256,1024]{1,0:T(8,128)(2,1)} %slice.2432), channel_id=1, source_target_pairs={{0,4},{4,0},{1,5},{5,1},{2,6},{6,2},{3,7},{7,3},{8,12},{12,8},{9,1... | collective-permute-start | bytes 1572872 | tf_op jit(solution)/shard_map/ppermute | solution.py:47
  440.7 70.3 %collective-permute-start.47 = (bf16[1,2,2,2,64,768]{5,4,3,2,1,0:T(8,128)(2,1)}, bf16[1,2,2,2,64,768]{5,4,3,2,1,0:T(8,128)(2,1)}, u32[]{:S(2)}, u32[]{:S(2)}) collective-permute-start(bf16[1,2,2,2,64,768]{5,4,3,2,1,0:T(8,128)(2,1)} %bitcast.54), channel_id=1, source_target_pairs={{0,32},{32,0},{64,96},{96,64},{1,33},{33,1},{65,97},{97,65},{2,34}... | collective-permute-start | bytes 2359304 | tf_op jit(solution)/shard_map/ppermute | solution.py:83
  444.3 49.8 %collective-permute-start.48 = (bf16[2,1,2,2,64,768]{5,4,3,2,1,0:T(8,128)(2,1)}, bf16[2,1,2,2,64,768]{5,4,3,2,1,0:T(8,128)(2,1)}, u32[]{:S(2)}, u32[]{:S(2)}) collective-permute-start(bf16[2,1,2,2,64,768]{5,4,3,2,1,0:T(8,128)(2,1)} %slice.1382), channel_id=1, source_target_pairs={{0,8},{8,0},{16,24},{24,16},{1,9},{9,1},{17,25},{25,17},{2,10},{10... | collective-permute-start | bytes 2359304 | tf_op jit(solution)/shard_map/ppermute | solution.py:83
  454.0 21.8 %collective-permute-start.67 = (bf16[1,1,2,2,64,1152]{5,4,3,2,1,0:T(8,128)(2,1)}, bf16[1,1,2,2,64,1152]{5,4,3,2,1,0:T(8,128)(2,1)}, u32[]{:S(2)}, u32[]{:S(2)}) collective-permute-start(bf16[1,1,2,2,64,1152]{5,4,3,2,1,0:T(8,128)(2,1)} %slice.1105), channel_id=1, source_target_pairs={{0,8},{8,0},{16,24},{24,16},{1,9},{9,1},{17,25},{25,17},{2,10},{10... | collective-permute-start | bytes 1769480 | tf_op jit(solution)/shard_map/ppermute | solution.py:83
  494.1 20.5 %collective-permute-start.71 = (bf16[1,1,1,2,64,1152]{5,4,3,2,1,0:T(8,128)(2,1)S(1)}, bf16[1,1,1,2,64,1152]{5,4,3,2,1,0:T(8,128)(2,1)S(1)}, u32[]{:S(2)}, u32[]{:S(2)}) collective-permute-start(bf16[1,1,1,2,64,1152]{5,4,3,2,1,0:T(8,128)(2,1)S(1)} %slice.1113), channel_id=1, source_target_pairs={{0,96},{96,0},{32,64},{64,32},{1,97},{97,1},{33,65},{65,33},{2,98}... | collective-permute-start | bytes 884744 | tf_op jit(solution)/shard_map/ppermute | solution.py:83
  509.9 23.3 %collective-permute-start.73 = (bf16[1,2,1,1,64,1152]{5,4,3,2,1,0:T(8,128)(2,1)S(1)}, bf16[1,2,1,1,64,1152]{5,4,3,2,1,0:T(8,128)(2,1)S(1)}, u32[]{:S(2)}, u32[]{:S(2)}) collective-permute-start(bf16[1,2,1,1,64,1152]{5,4,3,2,1,0:T(8,128)(2,1)S(1)} %slice.1117), channel_id=1, source_target_pairs={{0,32},{32,0},{64,96},{96,64},{1,33},{33,1},{65,97},{97,65},{2,34}... | collective-permute-start | bytes 884744 | tf_op jit(solution)/shard_map/ppermute | solution.py:83
  510.9 32.4 %collective-permute-start.74 = (bf16[1,1,2,1,64,1152]{5,4,3,2,1,0:T(8,128)(2,1)S(1)}, bf16[1,1,2,1,64,1152]{5,4,3,2,1,0:T(8,128)(2,1)S(1)}, u32[]{:S(2)}, u32[]{:S(2)}) collective-permute-start(bf16[1,1,2,1,64,1152]{5,4,3,2,1,0:T(8,128)(2,1)S(1)} %slice.1119), channel_id=1, source_target_pairs={{0,8},{8,0},{16,24},{24,16},{1,9},{9,1},{17,25},{25,17},{2,10},{10... | collective-permute-start | bytes 884744 | tf_op jit(solution)/shard_map/ppermute | solution.py:83
  (171 other events, 2175.7 us)
